TPU v7x, 32 devices: a whole 2x2x4 slice. The times are simulated.
32 devices in a mesh: groups: 2 (over x), chan: 16 (over z, y, core).
Axes of the slice: x: 2, y: 2, z: 4, core: 2. Of those that a mesh axis runs over, the one named last changes fastest.
Arguments:
- raw_strain: bfloat16 [8, 512, 4096], P(None, ('groups', 'chan')), parts along dimension 1, may hold values from -60 to 60
- bandpass: bfloat16 [64], replicated, may hold values from -0.75 to 0.75
- whiten_taps: bfloat16 [512, 64], P(('groups', 'chan')), parts along dimension 0, may hold values from -0.75 to 0.75
- segment_mask: int32 [8, 512], P(None, 'groups'), parts along dimension 1, may hold values from 0 to 1, as said below
- channel_block: int32 [512], P('groups'), parts along dimension 0, may hold values from 0 to 1, as said below
- source_block: int32 [2], P('groups'), parts along dimension 0, may hold values from 0 to 1
Outputs:
- correlations: bfloat16 [128, 512, 1024], P(None, ('groups', 'chan')), parts along dimension 1
There are 2 independent parts, one for each index of `groups`. A program takes and returns all parts, laid end to end along the dimension named above; an argument that names none is the same for every part. Nothing has to cross between parts.
Inputs may be any that keep to these rules, and one draw needn't show every extreme that they name: `segment_mask`: 1 marks a usable segment of a channel; some channels have no usable segment. `channel_block`: each block number is held by exactly 128 channels.
All inputs are finite; a program needn't handle non-finite values.
Results may differ from a plain program's by a relative error of at most 0.0093.
Values may be sent and summed in bfloat16 or wider, within the bound.
A program may use at most 64 MiB of HBM per device.

v0:
```python
import functools
import math

import jax
import numpy as np
import jax.numpy as jnp
from jax import lax
from jax.experimental import pallas as pl
from jax.experimental.pallas import tpu as pltpu
from jax.sharding import PartitionSpec as P

SAMPLES = 4096
KLO = 64
FBINS = 512
LAGS = 1024
BLOCK = 128


def table(phase):
    angles = phase.astype(np.float32) * np.float32(2.0 * math.pi / SAMPLES)
    return np.cos(angles).astype(jnp.bfloat16), (-np.sin(angles)).astype(jnp.bfloat16)


def bin_order():
    bins = KLO + np.arange(FBINS)
    return np.concatenate([bins[bins % 2 == 0], bins[bins % 2 == 1]])


def dft_table():
    even, odd = np.split(bin_order(), 2)
    time = np.arange(SAMPLES // 2)[:, None]
    return np.concatenate(table(time * even % SAMPLES) + table(time * odd % SAMPLES), axis=1)


def lag_table_np():
    return np.concatenate(table(bin_order()[:, None] * (np.arange(LAGS) - LAGS // 2)[None, :] % SAMPLES), axis=0)


def toeplitz(taps):
    turned = pltpu.roll(jnp.broadcast_to(taps, (128, 128)), 0, 1, stride=1, stride_axis=0)
    row = lax.broadcasted_iota(jnp.int32, (128, 128), 0)
    lane = lax.broadcasted_iota(jnp.int32, (128, 128), 1)
    before = jnp.where(lane < row, turned, 0.0)
    here = jnp.where(lane >= row, turned, 0.0)
    return jnp.concatenate([before, here], axis=0).astype(jnp.bfloat16)


def front_kernel(raw_ref, band_ref, taps_ref, mask_ref, table_ref, out_ref, filt, inv, white, acc):
    segs, rows, samples = raw_ref.shape
    blocks = samples // 128
    step = pl.program_id(0)
    depth = table_ref.shape[0]

    @pl.when(step == 0)
    def _():
        widen = lambda x: jnp.pad(x.astype(jnp.float32), ((0, 0), (0, 128 - x.shape[1])))
        matrix = toeplitz(widen(band_ref[...]))
        taps = widen(taps_ref[...])
        power = jnp.zeros((segs * rows, 128), jnp.float32)
        for b in range(blocks):
            if b == 0:
                joined = jnp.concatenate([raw_ref[:, :, samples - 128 :], raw_ref[:, :, :128]], axis=2)
            else:
                joined = raw_ref[:, :, (b - 1) * 128 : (b + 1) * 128]
            part = jnp.dot(joined.reshape(segs * rows, 256), matrix, preferred_element_type=jnp.float32)
            power = power + part * part
            filt[:, :, b * 128 : (b + 1) * 128] = part.reshape(segs, rows, 128)
        energy = jnp.sum(power, axis=1, keepdims=True) * (1.0 / samples)
        scale = 1.0 / jnp.sqrt(energy + 1e-05)
        inv[...] = jnp.broadcast_to(scale, (segs * rows, 128)).reshape(segs, rows, 128)
        for c in range(rows):
            matrix = toeplitz(taps[c : c + 1, :])
            scale = inv[:, c, :]
            here = jnp.concatenate(
                [filt[:, c, b * 128 : (b + 1) * 128] * scale for b in range(blocks)], axis=0
            )
            before = jnp.concatenate([here[-segs:], here[:-segs]], axis=0)
            joined = jnp.concatenate([before, here], axis=1).astype(jnp.bfloat16)
            part = jnp.dot(joined, matrix, preferred_element_type=jnp.float32)
            for b in range(blocks):
                white[c * segs : (c + 1) * segs, b * 128 : (b + 1) * 128] = part[b * segs : (b + 1) * segs]
        acc[...] = jnp.zeros_like(acc)

    first = pl.multiple_of(step * depth, depth)
    early = white[:, pl.ds(first, depth)].astype(jnp.bfloat16).astype(jnp.float32)
    late = white[:, pl.ds(pl.multiple_of(first + samples // 2, depth), depth)].astype(jnp.bfloat16).astype(jnp.float32)
    for odd, folded in enumerate((early + late, early - late)):
        part = jnp.dot(
            folded.astype(jnp.bfloat16),
            table_ref[:, odd * FBINS : (odd + 1) * FBINS],
            preferred_element_type=jnp.float32,
        )
        half = FBINS // 2
        acc[:, odd * half : (odd + 1) * half] += part[:, :half]
        acc[:, FBINS + odd * half : FBINS + (odd + 1) * half] += part[:, half:]

    @pl.when(step == pl.num_programs(0) - 1)
    def _():
        out_ref[...] = (acc[...] * mask_ref[...]).astype(jnp.bfloat16)


def front(raw, bandpass, whiten_taps, mask_here):
    segs, rows, samples = raw.shape
    band, taps = bandpass[None], whiten_taps
    mask = mask_here.T.reshape(rows * segs, 1)
    depth = 512
    whole = lambda *shape: pl.BlockSpec(shape, lambda i: (0,) * len(shape))
    return pl.pallas_call(
        front_kernel,
        grid=(samples // 2 // depth,),
        out_shape=jax.ShapeDtypeStruct((rows * segs, 2 * FBINS), jnp.bfloat16),
        in_specs=[
            whole(segs, rows, samples),
            whole(*band.shape),
            whole(*taps.shape),
            whole(rows * segs, 1),
            pl.BlockSpec((depth, 2 * FBINS), lambda i: (i, 0)),
        ],
        out_specs=whole(rows * segs, 2 * FBINS),
        scratch_shapes=[
            pltpu.VMEM((segs, rows, samples), jnp.float32),
            pltpu.VMEM((segs, rows, 128), jnp.float32),
            pltpu.VMEM((rows * segs, samples), jnp.float32),
            pltpu.VMEM((rows * segs, 2 * FBINS), jnp.float32),
        ],
        compiler_params=pltpu.CompilerParams(vmem_limit_bytes=40 * 2**20),
        cost_estimate=pl.CostEstimate(flops=2 * 10**9, bytes_accessed=10**7, transcendentals=0),
    )(raw, band, taps, mask, jnp.asarray(dft_table()))


PIECES = 2


def gather_kernel(count, own_ref, out_ref, own_sem, up_sem, down_sem, y_sem, core_sem, recv_sem):
    levels = count // 4
    me = lax.axis_index("chan")
    level, side, core = me // 4, (me // 2) % 2, me % 2
    y_peer = me + 2 - 4 * side
    core_peer = me + 1 - 2 * core
    has_up, has_down = level < levels - 1, level > 0
    barrier = pltpu.get_barrier_semaphore()

    def greet(peer):
        pl.semaphore_signal(barrier, inc=1, device_id={"chan": peer}, device_id_type=pl.DeviceIdType.MESH)

    greet(y_peer)
    greet(core_peer)

    @pl.when(has_up)
    def _():
        greet(me + 4)

    @pl.when(has_down)
    def _():
        greet(me - 4)

    pl.semaphore_wait(barrier, 2 + has_up.astype(jnp.int32) + has_down.astype(jnp.int32))

    height = own_ref.shape[0] // PIECES

    def send(block, piece, sems, peer, source=None):
        rows = pl.ds(piece * height, height)
        place = out_ref.at[block, rows]
        return pltpu.make_async_remote_copy(
            src_ref=place if source is None else source.at[rows],
            dst_ref=place,
            send_sem=sems.at[block, piece],
            recv_sem=recv_sem.at[block, piece],
            device_id={"chan": peer},
            device_id_type=pl.DeviceIdType.MESH,
        )

    def arrived(block, piece):
        send(block, piece, y_sem, y_peer).wait_recv()

    keep = pltpu.make_async_copy(own_ref, out_ref.at[me], own_sem)
    keep.start()
    for piece in range(PIECES):

        @pl.when(has_up)
        def _():
            send(me, piece, up_sem, me + 4, own_ref).start()

        @pl.when(has_down)
        def _():
            send(me, piece, down_sem, me - 4, own_ref).start()

        send(me, piece, y_sem, y_peer, own_ref).start()
        send(me, piece, core_sem, core_peer, own_ref).start()

    def across(far, way, piece):
        block = far * 4 + (1 - side) * 2 + core
        arrived(block, piece)
        send(block, piece, core_sem, core_peer).start()

    def along(far, way, piece):
        block = far * 4 + side * 2 + core
        arrived(block, piece)

        @pl.when(has_down if way == 1 else has_up)
        def _():
            sems, peer = (down_sem, me - 4) if way == 1 else (up_sem, me + 4)
            send(block, piece, sems, peer).start()

        send(block, piece, y_sem, y_peer).start()
        send(block, piece, core_sem, core_peer).start()

    def each(distance, piece, act):
        for way in (1, -1) if distance else (1,):
            far = level + way * distance

            @pl.when((far >= 0) & (far < levels))
            def _():
                act(far, way, piece)

    for distance in range(1, levels + 1):
        for piece in range(PIECES):
            if distance < levels:
                each(distance, piece, along)
            each(distance - 1, piece, across)

    for far in range(levels):
        for piece in range(PIECES):
            mine, other = far * 4 + side * 2 + core, far * 4 + (1 - side) * 2 + core
            arrived(far * 4 + side * 2 + 1 - core, piece)
            arrived(far * 4 + (1 - side) * 2 + 1 - core, piece)
            send(mine, piece, y_sem, y_peer).wait_send()
            send(mine, piece, core_sem, core_peer).wait_send()
            send(other, piece, core_sem, core_peer).wait_send()

            @pl.when(has_up & (far <= level))
            def _():
                send(mine, piece, up_sem, me + 4).wait_send()

            @pl.when(has_down & (far >= level))
            def _():
                send(mine, piece, down_sem, me - 4).wait_send()

    keep.wait()


def gather(own, count):
    if count % 4 or count < 4:
        return lax.all_gather(own, "chan", axis=0)
    sems = pltpu.SemaphoreType.DMA((count, PIECES))
    return pl.pallas_call(
        lambda *refs: gather_kernel(count, *refs),
        out_shape=jax.ShapeDtypeStruct((count,) + own.shape, own.dtype),
        in_specs=[pl.BlockSpec(memory_space=pltpu.VMEM)],
        out_specs=pl.BlockSpec(memory_space=pltpu.VMEM),
        scratch_shapes=[pltpu.SemaphoreType.DMA, sems, sems, sems, sems, sems],
        compiler_params=pltpu.CompilerParams(
            collective_id=0, has_side_effects=True, vmem_limit_bytes=40 * 2**20
        ),
    )(own)


CHUNK = 16
SOURCES_STEP = 2 * CHUNK


def back_kernel(index_ref, all_ref, own_ref, scale_ref, lag_ref, out_ref, local, first, stacked_a, stacked_b):
    rows, segs = local.shape[1], local.shape[0]
    step = pl.program_id(0)

    @pl.when(step == 0)
    def _():
        for r in range(0, rows, 2):
            pair = own_ref[r * segs : (r + 2) * segs].astype(jnp.float32)
            for k in range(2):
                for g in range(segs):
                    local[g, r + k : r + k + 1, :] = pair[k * segs + g : k * segs + g + 1]

    for chunk, stacked in enumerate((stacked_a, stacked_b)):
        base = chunk * CHUNK
        for s in range(CHUNK):
            channel = index_ref[step * SOURCES_STEP + base + s]
            pair = all_ref[pl.ds(pl.multiple_of((channel // 2) * 2 * segs, 2 * segs), 2 * segs), :]
            pair = pair.astype(jnp.float32)
            first[base + s] = jnp.where(channel % 2 == 0, pair[:segs], pair[segs:])
        for j in range(FBINS // 128):
            re, im = slice(j * 128, (j + 1) * 128), slice(FBINS + j * 128, FBINS + (j + 1) * 128)
            far = [(local[g, :, re], local[g, :, im]) for g in range(segs)]
            for s in range(CHUNK):
                total_re, total_im = 0.0, 0.0
                for g in range(segs):
                    a = jnp.broadcast_to(first[base + s, g : g + 1, re], (rows, 128))
                    b = jnp.broadcast_to(first[base + s, g : g + 1, im], (rows, 128))
                    total_re = total_re + a * far[g][0] + b * far[g][1]
                    total_im = total_im + a * far[g][1] - b * far[g][0]
                stacked[s * rows : (s + 1) * rows, re] = total_re.astype(jnp.bfloat16)
                stacked[s * rows : (s + 1) * rows, im] = total_im.astype(jnp.bfloat16)
        lagged = jnp.dot(stacked[...], lag_ref[...], preferred_element_type=jnp.float32)
        lagged = lagged * scale_ref[base * rows : (base + CHUNK) * rows]
        out_ref[base : base + CHUNK] = lagged.astype(jnp.bfloat16).reshape(CHUNK, rows, LAGS)


def back(index, gathered, own, scale, rows, segs):
    width = 2 * FBINS
    once = lambda *shape: pl.BlockSpec(
        shape, lambda i, *_: (0,) * len(shape), pipeline_mode=pl.Buffered(1)
    )
    return pl.pallas_call(
        back_kernel,
        out_shape=jax.ShapeDtypeStruct((BLOCK, rows, LAGS), jnp.bfloat16),
        grid_spec=pltpu.PrefetchScalarGridSpec(
            num_scalar_prefetch=1,
            grid=(BLOCK // SOURCES_STEP,),
            in_specs=[
                once(*gathered.shape),
                once(*own.shape),
                pl.BlockSpec((SOURCES_STEP * rows, 1), lambda i, *_: (i, 0)),
                once(width, LAGS),
            ],
            out_specs=pl.BlockSpec((SOURCES_STEP, rows, LAGS), lambda i, *_: (i, 0, 0)),
            scratch_shapes=[
                pltpu.VMEM((segs, rows, width), jnp.float32),
                pltpu.VMEM((SOURCES_STEP, segs, width), jnp.float32),
                pltpu.VMEM((CHUNK * rows, width), jnp.bfloat16),
                pltpu.VMEM((CHUNK * rows, width), jnp.bfloat16),
            ],
        ),
        compiler_params=pltpu.CompilerParams(vmem_limit_bytes=44 * 2**20),
        cost_estimate=pl.CostEstimate(flops=5 * 10**9, bytes_accessed=10**7, transcendentals=0),
    )(index, gathered, own, scale, jnp.asarray(lag_table_np()))


def body(chan_count, raw_strain, bandpass, whiten_taps, segment_mask, channel_block, source_block):
    seg_count, chan_rows, sample_count = raw_strain.shape
    chan_start = lax.axis_index("chan") * chan_rows
    mask_all = segment_mask.astype(jnp.float32)
    mask_here = lax.dynamic_slice_in_dim(mask_all, chan_start, chan_rows, 1)
    spectra = front(raw_strain, bandpass, whiten_taps, mask_here)
    gathered = gather(spectra, chan_count).reshape(-1, 2 * FBINS)
    member = channel_block == source_block[0]
    order = jnp.arange(member.shape[0], dtype=jnp.int32)
    below = member[None, :] & (order[None, :] < order[:, None])
    member_rank = jnp.sum(below.astype(jnp.int32), axis=1)
    chosen = member[None, :] & (member_rank[None, :] == jnp.arange(BLOCK, dtype=jnp.int32)[:, None])
    index = jnp.sum(jnp.where(chosen, order[None, :], 0), axis=1)
    source_mask = jnp.dot(mask_all, chosen.astype(jnp.float32).T)
    counts = jnp.dot(source_mask.T, mask_here)
    factor = 2.0 / (SAMPLES * math.sqrt(FBINS))
    scale = (factor / jnp.maximum(counts, 1.0)).reshape(BLOCK * chan_rows, 1)
    return back(index, gathered, spectra, scale, chan_rows, seg_count)


def solution(mesh):
    in_specs = (
        P(None, ("groups", "chan"), None),
        P(),
        P(("groups", "chan"), None),
        P(None, "groups"),
        P("groups"),
        P("groups"),
    )
    out_specs = P(None, ("groups", "chan"), None)
    return jax.shard_map(functools.partial(body, mesh.shape["chan"]), mesh=mesh, in_specs=in_specs, out_specs=out_specs, check_vma=False)
```

profile of v0, /device:TPU:1, one launch (start us, length us, event | category | flops | bytes accessed | tf_op | source)
XLA Modules:
  0.0 63.1 jit_solution(2433028192999866284)
XLA Ops:
  0.7 0.7 %broadcast_compare_fusion = pred[256]{0:T(512)(128)(4,1)S(1)} fusion(s32[256]{0:T(256)} %param.12, s32[]{:T(128)} %bitcast.6), kind=kLoop, calls=%fused_computation.13 | loop fusion | flops 256 | bytes 1284 | tf_op jit(solution)/shard_map/eq | solution.py:335
  1.3 0.1 convert_reduce_fusion
  1.5 0.1 select_reduce_fusion.index_ref
  1.6 0.7 %convert_element_type.8 = f32[8,256]{1,0:T(8,128)S(1)} convert(s32[8,256]{1,0:T(8,128)} %param.11) | non-fusion elementwise | flops 2048 | bytes 16384 | tf_op jit(solution)/shard_map/convert_element_type | solution.py:331
  2.3 0.1 dynamic-slice_bitcast_fusion
  2.4 0.3 fusion
  2.6 0.1 copy.16
  2.7 0.1 reshape.14.mask_ref
  2.8 0.1 copy.18
  2.9 0.0 copy-start
  2.9 1.2 %copy-done = bf16[8,16,4096]{2,1,0:T(8,128)(2,1)S(1)} copy-done((bf16[8,16,4096]{2,1,0:T(8,128)(2,1)S(1)}, bf16[8,16,4096]{2,1,0:T(8,128)(2,1)}, u32[]{:S(2)}) %copy-start) | copy-done | bytes 1048600
  4.1 0.0 copy-start.1
  4.1 0.7 %copy-done.1 = bf16[16,64]{1,0:T(8,128)(2,1)S(1)} copy-done((bf16[16,64]{1,0:T(8,128)(2,1)S(1)}, bf16[16,64]{1,0:T(8,128)(2,1)}, u32[]{:S(2)}) %copy-start.1) | copy-done | bytes 2072
  4.8 0.0 copy-start.2
  4.8 0.7 %copy-done.2 = bf16[64]{0:T(256)(128)(2,1)S(1)} copy-done((bf16[64]{0:T(256)(128)(2,1)S(1)}, bf16[64]{0:T(256)(128)(2,1)}, u32[]{:S(2)}) %copy-start.2) | copy-done | bytes 152
  5.5 0.0 copy-start.3
  5.5 2.2 %copy-done.3 = bf16[2048,1024]{1,0:T(8,128)(2,1)S(1)} copy-done((bf16[2048,1024]{1,0:T(8,128)(2,1)S(1)}, bf16[2048,1024]{1,0:T(8,128)(2,1)}, u32[]{:S(2)}) %copy-start.3) | copy-done | bytes 4194328
  7.7 4.5 %shard_map.82.refs_0_.own_ref = bf16[128,1024]{1,0:T(8,128)(2,1)S(1)} custom-call(bf16[8,16,4096]{2,1,0:T(8,128)(2,1)S(1)} %copy-done, bf16[1,64]{1,0:T(2,128)(2,1)S(1)} %bitcast.8, bf16[16,64]{1,0:T(8,128)(2,1)S(1)} %copy-done.1, f32[128,1]{1,0:T(8,128)S(1)} %reshape.14.mask_ref, bf16[2048,1024]{1,0:T(8,128)(2,1)S(1)} %copy-done.3), custom_call_target="tpu_custom_call" | custom-call | flops 2000000000 | bytes 10000000 | tf_op jit(solution)/shard_map/pallas_call | solution.py:108
  12.1 0.0 copy-start.4
  12.2 0.6 reshape.15.scale_ref
  12.7 29.9 %shard_map.83 = bf16[16,128,1024]{2,1,0:T(8,128)(2,1)S(1)} custom-call(bf16[128,1024]{1,0:T(8,128)(2,1)S(1)} %shard_map.82.refs_0_.own_ref), custom_call_target="tpu_custom_call" | custom-call | tf_op jit(solution)/shard_map/pallas_call | solution.py:246
  42.6 0.0 copy-done.4
  42.6 20.5 %shard_map.84 = bf16[128,16,1024]{2,1,0:T(8,128)(2,1)} custom-call(s32[128]{0:T(128)S(1)} %select_reduce_fusion.index_ref, bf16[2048,1024]{1,0:T(8,128)(2,1)S(1)} %bitcast.7, bf16[128,1024]{1,0:T(8,128)(2,1)S(1)} %shard_map.82.refs_0_.own_ref, f32[2048,1]{1,0:T(8,128)S(1)} %reshape.15.scale_ref, bf16[1024,1024]{1,0:T(8,128)(2,1)S(1)} %copy-done.4), custom_call_target="tpu_custom_call" | custom-call | flops 5000000000 | bytes 10000000 | tf_op jit(solution)/shard_map/pallas_call | solution.py:303
Async XLA Ops:
  2.9 1.2 %copy-start = (bf16[8,16,4096]{2,1,0:T(8,128)(2,1)S(1)}, bf16[8,16,4096]{2,1,0:T(8,128)(2,1)}, u32[]{:S(2)}) copy-start(bf16[8,16,4096]{2,1,0:T(8,128)(2,1)} %raw_ref.1) | copy-start | bytes 3145732
  4.1 0.7 %copy-start.1 = (bf16[16,64]{1,0:T(8,128)(2,1)S(1)}, bf16[16,64]{1,0:T(8,128)(2,1)}, u32[]{:S(2)}) copy-start(bf16[16,64]{1,0:T(8,128)(2,1)} %taps_ref.1) | copy-start | bytes 6148
  4.8 0.7 %copy-start.2 = (bf16[64]{0:T(256)(128)(2,1)S(1)}, bf16[64]{0:T(256)(128)(2,1)}, u32[]{:S(2)}) copy-start(bf16[64]{0:T(256)(128)(2,1)} %param.9) | copy-start | bytes 388
  5.5 2.2 %copy-start.3 = (bf16[2048,1024]{1,0:T(8,128)(2,1)S(1)}, bf16[2048,1024]{1,0:T(8,128)(2,1)}, u32[]{:S(2)}) copy-start(bf16[2048,1024]{1,0:T(8,128)(2,1)} %constant.18.clone.table_ref) | copy-start | bytes 12582916
  12.1 30.5 %copy-start.4 = (bf16[1024,1024]{1,0:T(8,128)(2,1)S(1)}, bf16[1024,1024]{1,0:T(8,128)(2,1)}, u32[]{:S(2)}) copy-start(bf16[1024,1024]{1,0:T(8,128)(2,1)} %constant.19.clone.lag_ref) | copy-start | bytes 6291460
where the time goes:
time: 63.5 us; the launch traced here: 63.1 us
  Pallas kernels  54.8 us (86%)
  local copies, waits for them, and re-layouts  5.66 us (9%)
  other arithmetic  1.62 us (3%)
  between operations  0.72 us (1%)
    pallas_call x1, Pallas kernels, gather(): pl.pallas_call(lambda *refs: gather_kernel(count, *refs), out_shape=jax.S...  29.9 us
    pallas_call x1, Pallas kernels, back(): pl.pallas_call(back_kernel, out_shape=jax.ShapeDtypeStruct((BLOCK, rows,...  20.5 us
    unnamed x10, local copies, waits for them, and re-layouts  4.76 us
    pallas_call x1, Pallas kernels, front(): pl.pallas_call(front_kernel, grid=(samples // 2 // depth,), out_shape=jax...  4.49 us

commit v1 on v0

v1 whole, which is shorter than its diff:
```python
import functools
import math

import jax
import numpy as np
import jax.numpy as jnp
from jax import lax
from jax.experimental import pallas as pl
from jax.experimental.pallas import tpu as pltpu
from jax.sharding import PartitionSpec as P

SAMPLES = 4096
KLO = 64
FBINS = 512
LAGS = 1024
BLOCK = 128
GROUP = 16
GROUPS = FBINS // GROUP
PIECES = 4
CROSS = 1
BATCH = 4
PIECE_KEY, HOP_KEY = 2, 2


def table(phase):
    angles = phase.astype(np.float32) * np.float32(2.0 * math.pi / SAMPLES)
    return np.cos(angles).astype(jnp.bfloat16), (-np.sin(angles)).astype(jnp.bfloat16)


def bin_order():
    bins = KLO + np.arange(FBINS)
    return np.concatenate([bins[bins % 2 == 0], bins[bins % 2 == 1]])


def dft_table():
    time = np.arange(SAMPLES // 2)[:, None]
    parts = [np.concatenate(table(time * bins[None, :] % SAMPLES), axis=1) for bins in np.split(bin_order(), 4)]
    return np.stack(parts)


def lag_table_np():
    bins = bin_order().reshape(GROUPS, GROUP)
    lags = (np.arange(LAGS) - LAGS // 2)[None, :]
    return np.concatenate([part for group in bins for part in table(group[:, None] * lags % SAMPLES)], axis=0)


def toeplitz(taps):
    turned = pltpu.roll(jnp.broadcast_to(taps, (128, 128)), 0, 1, stride=1, stride_axis=0)
    row = lax.broadcasted_iota(jnp.int32, (128, 128), 0)
    lane = lax.broadcasted_iota(jnp.int32, (128, 128), 1)
    before = jnp.where(lane < row, turned, 0.0)
    here = jnp.where(lane >= row, turned, 0.0)
    return jnp.concatenate([before, here], axis=0).astype(jnp.bfloat16)


def exchange(parts):
    parts = list(parts)
    lane = lax.broadcasted_iota(jnp.int32, parts[0].shape, 1)
    if parts[0].dtype == jnp.bfloat16:
        lane = lane.astype(jnp.int16)
    bit = len(parts) // 2
    while bit:
        width = bit * 128 // len(parts)
        upper = (lane & width) != 0
        for i in range(len(parts)):
            if i & bit:
                continue
            a, b = parts[i], parts[i | bit]
            parts[i] = jnp.where(upper, pltpu.roll(b, width, 1), a)
            parts[i | bit] = jnp.where(upper, b, pltpu.roll(a, 128 - width, 1))
        bit //= 2
    return parts


def iota(shape, dim):
    return lax.broadcasted_iota(jnp.int32, shape, dim)


def one_hot(condition):
    return jnp.where(condition, 1.0, 0.0).astype(jnp.bfloat16)


def dot(a, b):
    return jnp.dot(a, b, preferred_element_type=jnp.float32)


def dot_nt(a, b):
    return lax.dot_general(a, b, (((1,), (1,)), ((), ())), preferred_element_type=jnp.float32)


def main_kernel(
    count, raw_hbm, band_hbm, taps_hbm, mask_hbm, block_hbm, source_ref, table_hbm, out_hbm,
    band_ref, taps_ref, mask_ref, block_ref, raw_ref, table_ref, filt, inv, white, acc, gath, loc, bd, sel, scale, scr,
    out_ref, load_sem, out_sem, near_sem, far_sem, recv_sem, core_sem,
):
    segs, rows, samples = raw_ref.shape
    levels = count // 4
    channels = count * rows
    width = rows * 2 * GROUP
    per_piece = GROUPS // PIECES
    me = lax.axis_index("chan")
    level, side, core = me // 4, (me // 2) % 2, me % 2
    y_peer = me + 2 - 4 * side
    core_peer = me + 1 - 2 * core
    has_up, has_down = level < levels - 1, level > 0
    barrier = pltpu.get_barrier_semaphore()

    small_loads = [
        pltpu.make_async_copy(far, near, load_sem.at[5 + k])
        for k, (far, near) in enumerate(
            ((block_hbm, block_ref), (mask_hbm, mask_ref), (band_hbm, band_ref), (taps_hbm, taps_ref))
        )
    ]
    for load in small_loads:
        load.start()
    raw_load = pltpu.make_async_copy(raw_hbm, raw_ref, load_sem.at[0])
    raw_load.start()
    table_loads = [
        pltpu.make_async_copy(table_hbm.at[b], table_ref.at[b], load_sem.at[1 + b]) for b in range(4)
    ]
    for load in table_loads:
        load.start()

    def greet(peer):
        pl.semaphore_signal(barrier, inc=1, device_id={"chan": peer}, device_id_type=pl.DeviceIdType.MESH)

    greet(y_peer)
    greet(core_peer)

    @pl.when(has_up)
    def _():
        greet(me + 4)

    @pl.when(has_down)
    def _():
        greet(me - 4)

    for load in small_loads:
        load.wait()
    member = block_ref[...] == source_ref[0]
    before = one_hot(iota((channels, channels), 0) < iota((channels, channels), 1))
    rank = dot(jnp.broadcast_to(one_hot(member), (8, channels)), before)[:1]
    chosen = member & (rank.astype(jnp.int32) == iota((BLOCK, channels), 0))
    picks = one_hot(chosen)
    sel[...] = picks
    mask = mask_ref[...].astype(jnp.float32).astype(jnp.bfloat16)
    spread = one_hot(iota((channels, width), 0) == me * rows + iota((channels, width), 1) // (2 * GROUP))
    mask_rows = dot(mask, spread)
    source_mask = dot_nt(picks, mask).astype(jnp.bfloat16)
    counts = dot(source_mask, mask_rows.astype(jnp.bfloat16))
    scale[...] = (2.0 / (SAMPLES * math.sqrt(FBINS))) / jnp.maximum(counts, 1.0)
    here = one_hot(iota((rows, channels), 1) == me * rows + iota((rows, channels), 0))
    mask_here = dot_nt(here, mask).astype(jnp.bfloat16)
    mask_segs = dot(mask_here, one_hot(iota((segs, 128), 0) == iota((segs, 128), 1) // GROUP))

    widen = lambda x: jnp.pad(x.astype(jnp.float32), ((0, 0), (0, 128 - x.shape[1])))
    matrix = toeplitz(widen(band_ref[...]))
    taps = widen(taps_ref[...])
    blocks = samples // 128
    raw_load.wait()
    power = jnp.zeros((segs * rows, 128), jnp.float32)
    for b in range(blocks):
        if b == 0:
            joined = jnp.concatenate([raw_ref[:, :, samples - 128 :], raw_ref[:, :, :128]], axis=2)
        else:
            joined = raw_ref[:, :, (b - 1) * 128 : (b + 1) * 128]
        part = dot(joined.reshape(segs * rows, 256), matrix)
        power = power + part * part
        filt[:, :, b * 128 : (b + 1) * 128] = part.reshape(segs, rows, 128)
    energy = jnp.sum(power, axis=1, keepdims=True) * (1.0 / samples)
    inv[...] = jnp.broadcast_to(1.0 / jnp.sqrt(energy + 1e-05), (segs * rows, 128)).reshape(segs, rows, 128)
    for c in range(rows):
        matrix = toeplitz(taps[c : c + 1, :])
        gain = inv[:, c, :]
        now = jnp.concatenate([filt[:, c, b * 128 : (b + 1) * 128] * gain for b in range(blocks)], axis=0)
        past = jnp.concatenate([now[-segs:], now[:-segs]], axis=0)
        part = dot(jnp.concatenate([past, now], axis=1).astype(jnp.bfloat16), matrix)
        for b in range(blocks):
            white[c * segs : (c + 1) * segs, b * 128 : (b + 1) * 128] = part[b * segs : (b + 1) * segs]

    pl.semaphore_wait(barrier, 2 + has_up.astype(jnp.int32) + has_down.astype(jnp.int32))

    def place(block, piece, blocks=1):
        first = block * rows if isinstance(block, int) else pl.multiple_of(block * rows, rows)
        return gath.at[piece, pl.ds(first, blocks * rows)]

    def copy(block, piece, sent, got, peer, blocks=1):
        return pltpu.make_async_remote_copy(
            src_ref=place(block, piece, blocks),
            dst_ref=place(block, piece, blocks),
            send_sem=sent.at[piece],
            recv_sem=got,
            device_id={"chan": peer},
            device_id_type=pl.DeviceIdType.MESH,
        )

    def to_core(block, piece):
        copy(block, piece, near_sem, core_sem.at[piece], core_peer).start()

    def to_y(far, piece):
        copy(far * 4 + side * 2 + core, piece, near_sem, recv_sem.at[far * 2 + 1, piece], y_peer).start()

    def to_z(far, other, piece, up):
        block = far * 4 + (1 - side if other else side) * 2 + core

        @pl.when(has_up if up else has_down)
        def _():
            copy(block, piece, far_sem, recv_sem.at[far * 2 + other, piece], me + 4 if up else me - 4).start()

    def arrived(far, other, piece):
        copy(me, piece, near_sem, recv_sem.at[far * 2 + other, piece], y_peer).wait_recv()

    def send_own(piece):
        to_z(level, 0, piece, True)
        to_z(level, 0, piece, False)
        to_y(level, piece)
        to_core(me, piece)

    def along(far, way, piece):
        arrived(far, 0, piece)
        to_z(far, 0, piece, way < 0)
        if piece >= CROSS:
            to_y(far, piece)
        to_core(far * 4 + side * 2 + core, piece)

    def across(far, way, piece):
        arrived(far, 1, piece)
        if piece < CROSS:
            if way >= 0:
                to_z(far, 1, piece, False)
            if way <= 0:
                to_z(far, 1, piece, True)
        to_core(far * 4 + (1 - side) * 2 + core, piece)

    def each(distance, piece, act):
        if distance == 0:
            act(level, 0, piece)
            return
        for way in (1, -1):
            far = level + way * distance

            @pl.when((far >= 0) & (far < levels))
            def _():
                act(far, way, piece)

    half = samples // 2
    mine = pl.ds(pl.multiple_of(me * rows, rows), rows)
    for b in range(4):
        if b % 2 == 0:
            early = white[:, :half].astype(jnp.bfloat16).astype(jnp.float32)
            late = white[:, half:].astype(jnp.bfloat16).astype(jnp.float32)
            folded = (early + late if b == 0 else early - late).astype(jnp.bfloat16)
        table_loads[b].wait()
        spectra = dot(folded, table_ref[b])
        for part in range(2):
            acc[b, part] = spectra[:, part * 128 : (part + 1) * 128]
            for k, value in enumerate(exchange([acc[b, part, pl.ds(g, rows, stride=segs), :] for g in range(segs)])):
                group = 8 * b + k
                first = group % per_piece * 256 + part * 128
                gath[group // per_piece, mine, first : first + 128] = (value * mask_segs).astype(jnp.bfloat16)
        for piece in range(b * PIECES // 4, (b + 1) * PIECES // 4):
            send_own(piece)

    for b in range(4):
        for tile in range(width // 128):
            own = [
                [acc[b, part, r * segs : (r + 1) * segs, :] for part in range(2)] for r in range(tile * 4, tile * 4 + 4)
            ]
            lanes = slice(tile * 128, (tile + 1) * 128)
            for kind, parts in enumerate(([x for re, im in own for x in (re, im)], [x for re, im in own for x in (im, -re)])):
                for k, value in enumerate(exchange(parts)):
                    loc[b * 8 + k, kind, :, lanes] = value * mask_rows[:, lanes]

    def build(group, carry):
        same = iota((GROUP, width), 0) == iota((GROUP, width), 1) % GROUP
        for kind in range(2):
            for g in range(segs):
                value = jnp.where(same, jnp.broadcast_to(loc[group, kind, g : g + 1, :], (GROUP, width)), 0.0)
                first = (kind * segs + g) * GROUP
                bd[group, first : first + GROUP, :] = value.astype(jnp.bfloat16)
        return carry

    lax.fori_loop(0, GROUPS, build, 0)

    def store(batch):
        return pltpu.make_async_copy(out_ref.at[batch], out_hbm.at[batch], out_sem.at[batch])

    def compute(piece):
        copy(0, piece, near_sem, core_sem.at[piece], core_peer, 2 * levels).wait_recv()

        def batch(index, carry):
            lanes = pl.ds(pl.multiple_of(index * BATCH * 256, BATCH * 256), BATCH * 256)
            sources = dot(sel[...], gath[piece, :, lanes]).astype(jnp.bfloat16)
            here = piece * (per_piece // BATCH) + index
            crossed = [dot(sources[:, k * 256 : (k + 1) * 256], bd[here * BATCH + k]) for k in range(BATCH)]
            for tile in range(width // 128):
                lanes = slice(tile * 128, (tile + 1) * 128)
                parts = exchange([(value[:, lanes] * scale[:, lanes]).astype(jnp.bfloat16) for value in crossed])
                for k, value in enumerate(parts):
                    scr[pl.ds(tile * 4 + k, BLOCK, stride=rows), :] = value.astype(jnp.float32)
            out_ref[here] = scr[...].astype(jnp.bfloat16)
            store(here).start()
            return carry

        lax.fori_loop(0, per_piece // BATCH, batch, 0)

    events = []
    for piece in range(PIECES):
        for distance in range(levels):
            if distance:
                events.append((piece * PIECE_KEY + distance * HOP_KEY, piece, distance, along))
            events.append((piece * PIECE_KEY + (distance + 1) * HOP_KEY, piece, distance, across))
        events.append((piece * PIECE_KEY + (levels + 1) * HOP_KEY, piece, -1, None))
    for _, piece, distance, act in sorted(events, key=lambda event: event[:3]):
        if act is None:
            compute(piece)
        else:
            each(distance, piece, act)

    for piece in range(PIECES):
        crossing = piece < CROSS
        copy(0, piece, near_sem, core_sem.at[piece], core_peer, 2 * levels + (1 if crossing else levels)).wait_send()
        each_way = 2 if crossing else 1

        @pl.when(has_up & has_down)
        def _():
            copy(0, piece, far_sem, core_sem.at[piece], core_peer, each_way * (levels + 1)).wait_send()

        @pl.when(has_up != has_down)
        def _():
            copy(0, piece, far_sem, core_sem.at[piece], core_peer, each_way).wait_send()

    for batch in range(GROUPS // BATCH):
        store(batch).wait()


def main(count, raw, bandpass, whiten_taps, segment_mask, channel_block, source_block):
    segs, rows, samples = raw.shape
    channels = count * rows
    hbm = pl.BlockSpec(memory_space=pltpu.HBM)
    return pl.pallas_call(
        functools.partial(main_kernel, count),
        out_shape=jax.ShapeDtypeStruct((GROUPS // BATCH, BLOCK * rows, 128), jnp.bfloat16),
        in_specs=[hbm, hbm, hbm, hbm, hbm, pl.BlockSpec(memory_space=pltpu.SMEM), hbm],
        out_specs=hbm,
        scratch_shapes=[
            pltpu.VMEM((1, bandpass.shape[0]), bandpass.dtype),
            pltpu.VMEM(whiten_taps.shape, whiten_taps.dtype),
            pltpu.VMEM(segment_mask.shape, segment_mask.dtype),
            pltpu.VMEM((1, channels), channel_block.dtype),
            pltpu.VMEM((segs, rows, samples), jnp.bfloat16),
            pltpu.VMEM((4, samples // 2, 256), jnp.bfloat16),
            pltpu.VMEM((segs, rows, samples), jnp.float32),
            pltpu.VMEM((segs, rows, 128), jnp.float32),
            pltpu.VMEM((rows * segs, samples), jnp.float32),
            pltpu.VMEM((4, 2, rows * segs, 128), jnp.float32),
            pltpu.VMEM((PIECES, channels, GROUPS // PIECES * 256), jnp.bfloat16),
            pltpu.VMEM((GROUPS, 2, segs, 2 * rows * GROUP), jnp.float32),
            pltpu.VMEM((GROUPS, 256, 2 * rows * GROUP), jnp.bfloat16),
            pltpu.VMEM((BLOCK, channels), jnp.bfloat16),
            pltpu.VMEM((BLOCK, 2 * rows * GROUP), jnp.float32),
            pltpu.VMEM((BLOCK * rows, 128), jnp.float32),
            pltpu.VMEM((GROUPS // BATCH, BLOCK * rows, 128), jnp.bfloat16),
            pltpu.SemaphoreType.DMA((9,)),
            pltpu.SemaphoreType.DMA((GROUPS // BATCH,)),
            pltpu.SemaphoreType.DMA((PIECES,)),
            pltpu.SemaphoreType.DMA((PIECES,)),
            pltpu.SemaphoreType.DMA((count // 2, PIECES)),
            pltpu.SemaphoreType.DMA((PIECES,)),
        ],
        compiler_params=pltpu.CompilerParams(
            collective_id=0, has_side_effects=True, vmem_limit_bytes=56 * 2**20
        ),
    )(raw, bandpass[None], whiten_taps, segment_mask, channel_block[None], source_block, jnp.asarray(dft_table()))


STEPS = 4


def lag_kernel(stacked_ref, lag_ref, out_ref):
    stacked = jnp.concatenate([stacked_ref[k] for k in range(stacked_ref.shape[0])], axis=1)
    lagged = dot(stacked, lag_ref[...])
    out_ref[...] = lagged.astype(jnp.bfloat16).reshape(out_ref.shape)


def lag(stacked, rows):
    return pl.pallas_call(
        lag_kernel,
        out_shape=jax.ShapeDtypeStruct((BLOCK, rows, LAGS), jnp.bfloat16),
        grid=(STEPS,),
        in_specs=[
            pl.BlockSpec((stacked.shape[0], BLOCK // STEPS * rows, 128), lambda i: (0, i, 0)),
            pl.BlockSpec(memory_space=pltpu.VMEM),
        ],
        out_specs=pl.BlockSpec((BLOCK // STEPS, rows, LAGS), lambda i: (i, 0, 0)),
        compiler_params=pltpu.CompilerParams(vmem_limit_bytes=58 * 2**20),
        cost_estimate=pl.CostEstimate(flops=4 * 10**9, bytes_accessed=10**7, transcendentals=0),
    )(stacked, jnp.asarray(lag_table_np()))


def body(count, raw_strain, bandpass, whiten_taps, segment_mask, channel_block, source_block):
    stacked = main(count, raw_strain, bandpass, whiten_taps, segment_mask, channel_block, source_block)
    return lag(stacked, raw_strain.shape[1])


def solution(mesh):
    in_specs = (
        P(None, ("groups", "chan"), None),
        P(),
        P(("groups", "chan"), None),
        P(None, "groups"),
        P("groups"),
        P("groups"),
    )
    out_specs = P(None, ("groups", "chan"), None)
    return jax.shard_map(functools.partial(body, mesh.shape["chan"]), mesh=mesh, in_specs=in_specs, out_specs=out_specs, check_vma=False)
```

time: 63.5 us -> 53.7 us (0.85)
  local copies, waits for them, and re-layouts: 5.66 us -> 0 us
  Pallas kernels: 54.8 us -> 52.9 us
  other arithmetic: 1.62 us -> 0 us
    unnamed x10 -> x0, local copies, waits for them, and re-layouts: 4.76 us -> none
    pallas_call x3 -> x2, Pallas kernels: 54.8 us -> 52.9 us  [the longest x1 44.5 us: main(): pl.pallas_call(functools.partial(main_kernel, count), out_shape=jax.Shape...]
    convert_element_type x1 -> x0, other arithmetic: 0.71 us -> none  [body(): mask_all = segment_mask.astype(jnp.float32)]
    eq x1 -> x0, other arithmetic: 0.69 us -> none  [body(): member = channel_block == source_block[0]]
    reshape x2 -> x0, local copies, waits for them, and re-layouts: 0.66 us -> none  [the longest x1 0.57 us: body(): scale = (factor / jnp.maximum(counts, 1.0)).reshape(BLOCK * chan_rows, 1)]
where the time goes in v1:
time: 53.7 us; the launch traced here: 53.5 us
  Pallas kernels  52.9 us (99%)
  between operations  0.66 us (1%)
    pallas_call x1, Pallas kernels, main(): pl.pallas_call(functools.partial(main_kernel, count), out_shape=jax.Shape...  44.5 us
    pallas_call x1, Pallas kernels, lag(): pl.pallas_call(lag_kernel, out_shape=jax.ShapeDtypeStruct((BLOCK, rows, L...  8.39 us

profile of v1, /device:TPU:1, one launch (start us, length us, event | category | flops | bytes accessed | tf_op | source)
XLA Modules:
  0.0 53.5 jit_solution(6900278290604091075)
XLA Ops:
  0.7 44.5 %shard_map.82.stacked_ref = bf16[8,2048,128]{2,1,0:T(8,128)(2,1)} custom-call(bf16[8,16,4096]{2,1,0:T(8,128)(2,1)} %raw_hbm.1, bf16[1,64]{1,0:T(2,128)(2,1)} %bitcast.3, bf16[16,64]{1,0:T(8,128)(2,1)} %taps_hbm.1, s32[8,256]{1,0:T(8,128)} %mask_hbm.1, s32[1,256]{1,0:T(1,128)} %bitcast.2, s32[1]{0:T(128)S(6)} %copy.9.source_ref, ...), custom_call_target="tpu_custom_call" | custom-call | tf_op jit(solution)/shard_map/pallas_call | solution.py:341
  45.2 8.4 %shard_map.83 = bf16[128,16,1024]{2,1,0:T(8,128)(2,1)} custom-call(bf16[8,2048,128]{2,1,0:T(8,128)(2,1)} %shard_map.82.stacked_ref, bf16[1024,1024]{1,0:T(8,128)(2,1)} %constant.5.clone.lag_ref), custom_call_target="tpu_custom_call" | custom-call | flops 4000000000 | bytes 10000000 | tf_op jit(solution)/shard_map/pallas_call | solution.py:387

commit v2 on v1

--- a/solution.py
+++ b/solution.py
@@ -16,10 +16,10 @@
 BLOCK = 128
 GROUP = 16
 GROUPS = FBINS // GROUP
-PIECES = 4
+PIECES = 8
 CROSS = 1
 BATCH = 4
-PIECE_KEY, HOP_KEY = 2, 2
+PIECE_KEY, HOP_KEY, COMPUTE_KEY = 1, 10, 1.5
 
 
 def table(phase):
@@ -310,7 +310,7 @@
             if distance:
                 events.append((piece * PIECE_KEY + distance * HOP_KEY, piece, distance, along))
             events.append((piece * PIECE_KEY + (distance + 1) * HOP_KEY, piece, distance, across))
-        events.append((piece * PIECE_KEY + (levels + 1) * HOP_KEY, piece, -1, None))
+        events.append((piece * PIECE_KEY + levels * HOP_KEY + COMPUTE_KEY, piece, -1, None))
     for _, piece, distance, act in sorted(events, key=lambda event: event[:3]):
         if act is None:
             compute(piece)
@@ -393,7 +393,7 @@
             pl.BlockSpec(memory_space=pltpu.VMEM),
         ],
         out_specs=pl.BlockSpec((BLOCK // STEPS, rows, LAGS), lambda i: (i, 0, 0)),
-        compiler_params=pltpu.CompilerParams(vmem_limit_bytes=58 * 2**20),
+        compiler_params=pltpu.CompilerParams(vmem_limit_bytes=50 * 2**20),
         cost_estimate=pl.CostEstimate(flops=4 * 10**9, bytes_accessed=10**7, transcendentals=0),
     )(stacked, jnp.asarray(lag_table_np()))
 

time: 53.7 us -> 47.6 us (0.89)
  Pallas kernels: 52.9 us -> 46.5 us
    pallas_call x1, Pallas kernels: 44.5 us -> 38.8 us  [main(): pl.pallas_call(functools.partial(main_kernel, count), out_shape=jax.Shape...]
    pallas_call x1, Pallas kernels: 8.39 us -> 7.68 us  [lag(): pl.pallas_call(lag_kernel, out_shape=jax.ShapeDtypeStruct((BLOCK, rows, L...]
where the time goes in v2:
time: 47.6 us; the launch traced here: 47.1 us
  Pallas kernels  46.5 us (98%)
  between operations  0.68 us (1%)
    pallas_call x1, Pallas kernels, main(): pl.pallas_call(functools.partial(main_kernel, count), out_shape=jax.Shape...  38.8 us
    pallas_call x1, Pallas kernels, lag(): pl.pallas_call(lag_kernel, out_shape=jax.ShapeDtypeStruct((BLOCK, rows, L...  7.68 us

profile of v2, /device:TPU:1, one launch (start us, length us, event | category | flops | bytes accessed | tf_op | source)
XLA Modules:
  0.0 47.1 jit_solution(2097554993750765229)
XLA Ops:
  0.7 0.0 copy-start
  0.7 38.8 %shard_map.82.stacked_ref = bf16[8,2048,128]{2,1,0:T(8,128)(2,1)} custom-call(bf16[8,16,4096]{2,1,0:T(8,128)(2,1)} %raw_hbm.1, bf16[1,64]{1,0:T(2,128)(2,1)} %bitcast.3, bf16[16,64]{1,0:T(8,128)(2,1)} %taps_hbm.1, s32[8,256]{1,0:T(8,128)} %mask_hbm.1, s32[1,256]{1,0:T(1,128)} %bitcast.2, s32[1]{0:T(128)S(6)} %copy.9.source_ref, ...), custom_call_target="tpu_custom_call" | custom-call | tf_op jit(solution)/shard_map/pallas_call | solution.py:341
  39.4 0.0 copy-done
  39.5 7.7 %shard_map.83 = bf16[128,16,1024]{2,1,0:T(8,128)(2,1)} custom-call(bf16[8,2048,128]{2,1,0:T(8,128)(2,1)} %shard_map.82.stacked_ref, bf16[1024,1024]{1,0:T(8,128)(2,1)S(1)} %copy-done), custom_call_target="tpu_custom_call" | custom-call | flops 4000000000 | bytes 10000000 | tf_op jit(solution)/shard_map/pallas_call | solution.py:387
Async XLA Ops:
  0.7 38.8 %copy-start = (bf16[1024,1024]{1,0:T(8,128)(2,1)S(1)}, bf16[1024,1024]{1,0:T(8,128)(2,1)}, u32[]{:S(2)}) copy-start(bf16[1024,1024]{1,0:T(8,128)(2,1)} %constant.5.clone.lag_ref) | copy-start | bytes 6291460

commit v3 on v2

--- a/solution.py
+++ b/solution.py
@@ -16,8 +16,9 @@
 BLOCK = 128
 GROUP = 16
 GROUPS = FBINS // GROUP
-PIECES = 8
+PIECES = 4
 CROSS = 1
+TOGETHER = 1
 BATCH = 4
 PIECE_KEY, HOP_KEY, COMPUTE_KEY = 1, 10, 1.5
 
@@ -90,7 +91,7 @@
 
 def main_kernel(
     count, raw_hbm, band_hbm, taps_hbm, mask_hbm, block_hbm, source_ref, table_hbm, out_hbm,
-    band_ref, taps_ref, mask_ref, block_ref, raw_ref, table_ref, filt, inv, white, acc, gath, loc, bd, sel, scale, scr,
+    band_ref, taps_ref, mask_ref, block_ref, raw_ref, table_ref, filt, inv, white, acc, gath, loc, bd, sel, scale,
     out_ref, load_sem, out_sem, near_sem, far_sem, recv_sem, core_sem,
 ):
     segs, rows, samples = raw_ref.shape
@@ -151,7 +152,7 @@
     scale[...] = (2.0 / (SAMPLES * math.sqrt(FBINS))) / jnp.maximum(counts, 1.0)
     here = one_hot(iota((rows, channels), 1) == me * rows + iota((rows, channels), 0))
     mask_here = dot_nt(here, mask).astype(jnp.bfloat16)
-    mask_segs = dot(mask_here, one_hot(iota((segs, 128), 0) == iota((segs, 128), 1) // GROUP))
+    mask_segs = dot(mask_here, one_hot(iota((segs, 128), 0) == iota((segs, 128), 1) // GROUP)).astype(jnp.bfloat16)
 
     widen = lambda x: jnp.pad(x.astype(jnp.float32), ((0, 0), (0, 128 - x.shape[1])))
     matrix = toeplitz(widen(band_ref[...]))
@@ -254,10 +255,11 @@
         spectra = dot(folded, table_ref[b])
         for part in range(2):
             acc[b, part] = spectra[:, part * 128 : (part + 1) * 128]
-            for k, value in enumerate(exchange([acc[b, part, pl.ds(g, rows, stride=segs), :] for g in range(segs)])):
+            own = [acc[b, part, pl.ds(g, rows, stride=segs), :].astype(jnp.bfloat16) for g in range(segs)]
+            for k, value in enumerate(exchange(own)):
                 group = 8 * b + k
                 first = group % per_piece * 256 + part * 128
-                gath[group // per_piece, mine, first : first + 128] = (value * mask_segs).astype(jnp.bfloat16)
+                gath[group // per_piece, mine, first : first + 128] = value * mask_segs
         for piece in range(b * PIECES // 4, (b + 1) * PIECES // 4):
             send_own(piece)
 
@@ -285,24 +287,27 @@
     def store(batch):
         return pltpu.make_async_copy(out_ref.at[batch], out_hbm.at[batch], out_sem.at[batch])
 
-    def compute(piece):
-        copy(0, piece, near_sem, core_sem.at[piece], core_peer, 2 * levels).wait_recv()
-
-        def batch(index, carry):
-            lanes = pl.ds(pl.multiple_of(index * BATCH * 256, BATCH * 256), BATCH * 256)
-            sources = dot(sel[...], gath[piece, :, lanes]).astype(jnp.bfloat16)
-            here = piece * (per_piece // BATCH) + index
-            crossed = [dot(sources[:, k * 256 : (k + 1) * 256], bd[here * BATCH + k]) for k in range(BATCH)]
-            for tile in range(width // 128):
-                lanes = slice(tile * 128, (tile + 1) * 128)
-                parts = exchange([(value[:, lanes] * scale[:, lanes]).astype(jnp.bfloat16) for value in crossed])
-                for k, value in enumerate(parts):
-                    scr[pl.ds(tile * 4 + k, BLOCK, stride=rows), :] = value.astype(jnp.float32)
-            out_ref[here] = scr[...].astype(jnp.bfloat16)
-            store(here).start()
-            return carry
-
-        lax.fori_loop(0, per_piece // BATCH, batch, 0)
+    def crossed(piece, batch):
+        lanes = slice(batch * BATCH * 256, (batch + 1) * BATCH * 256)
+        sources = dot(sel[...], gath[piece, :, lanes]).astype(jnp.bfloat16)
+        first = piece * per_piece + batch * BATCH
+        return [dot(sources[:, k * 256 : (k + 1) * 256], bd[first + k]) for k in range(BATCH)]
+
+    def arrange(values, batch):
+        parts = []
+        for tile in range(width // 128):
+            lanes = slice(tile * 128, (tile + 1) * 128)
+            parts += exchange([(value[:, lanes] * scale[:, lanes]).astype(jnp.bfloat16) for value in values])
+        out_ref[batch] = jnp.transpose(jnp.stack(parts), (1, 0, 2)).reshape(BLOCK * rows, 128)
+        store(batch).start()
+
+    def compute(pieces):
+        for piece in pieces:
+            copy(0, piece, near_sem, core_sem.at[piece], core_peer, 2 * levels).wait_recv()
+        batches = [(piece, batch) for piece in pieces for batch in range(per_piece // BATCH)]
+        values = [crossed(piece, batch) for piece, batch in batches]
+        for (piece, batch), value in zip(batches, values):
+            arrange(value, piece * (per_piece // BATCH) + batch)
 
     events = []
     for piece in range(PIECES):
@@ -310,10 +315,11 @@
             if distance:
                 events.append((piece * PIECE_KEY + distance * HOP_KEY, piece, distance, along))
             events.append((piece * PIECE_KEY + (distance + 1) * HOP_KEY, piece, distance, across))
-        events.append((piece * PIECE_KEY + levels * HOP_KEY + COMPUTE_KEY, piece, -1, None))
+        if piece % TOGETHER == TOGETHER - 1:
+            events.append((piece * PIECE_KEY + levels * HOP_KEY + COMPUTE_KEY, piece, -1, None))
     for _, piece, distance, act in sorted(events, key=lambda event: event[:3]):
         if act is None:
-            compute(piece)
+            compute(range(piece + 1 - TOGETHER, piece + 1))
         else:
             each(distance, piece, act)
 
@@ -359,7 +365,6 @@
             pltpu.VMEM((GROUPS, 256, 2 * rows * GROUP), jnp.bfloat16),
             pltpu.VMEM((BLOCK, channels), jnp.bfloat16),
             pltpu.VMEM((BLOCK, 2 * rows * GROUP), jnp.float32),
-            pltpu.VMEM((BLOCK * rows, 128), jnp.float32),
             pltpu.VMEM((GROUPS // BATCH, BLOCK * rows, 128), jnp.bfloat16),
             pltpu.SemaphoreType.DMA((9,)),
             pltpu.SemaphoreType.DMA((GROUPS // BATCH,)),

time: 47.6 us -> 45.9 us (0.964)
  Pallas kernels: 46.5 us -> 45 us
    pallas_call x1, Pallas kernels: 38.8 us -> 37.3 us  [main(): pl.pallas_call(functools.partial(main_kernel, count), out_shape=jax.Shape...]
where the time goes in v3:
time: 45.9 us; the launch traced here: 45.7 us
  Pallas kernels  45 us (98%)
  between operations  0.68 us (1%)
    pallas_call x1, Pallas kernels, main(): pl.pallas_call(functools.partial(main_kernel, count), out_shape=jax.Shape...  37.3 us
    pallas_call x1, Pallas kernels, lag(): pl.pallas_call(lag_kernel, out_shape=jax.ShapeDtypeStruct((BLOCK, rows, L...  7.68 us

profile of v3, /device:TPU:1, one launch (start us, length us, event | category | flops | bytes accessed | tf_op | source)
XLA Modules:
  0.0 45.7 jit_solution(4732217399275668977)
XLA Ops:
  0.7 0.0 copy-start
  0.7 37.3 %shard_map.82.stacked_ref = bf16[8,2048,128]{2,1,0:T(8,128)(2,1)} custom-call(bf16[8,16,4096]{2,1,0:T(8,128)(2,1)} %raw_hbm.1, bf16[1,64]{1,0:T(2,128)(2,1)} %bitcast.3, bf16[16,64]{1,0:T(8,128)(2,1)} %taps_hbm.1, s32[8,256]{1,0:T(8,128)} %mask_hbm.1, s32[1,256]{1,0:T(1,128)} %bitcast.2, s32[1]{0:T(128)S(6)} %copy.9.source_ref, ...), custom_call_target="tpu_custom_call" | custom-call | tf_op jit(solution)/shard_map/pallas_call | solution.py:347
  38.0 0.0 copy-done
  38.0 7.7 %shard_map.83 = bf16[128,16,1024]{2,1,0:T(8,128)(2,1)} custom-call(bf16[8,2048,128]{2,1,0:T(8,128)(2,1)} %shard_map.82.stacked_ref, bf16[1024,1024]{1,0:T(8,128)(2,1)S(1)} %copy-done), custom_call_target="tpu_custom_call" | custom-call | flops 4000000000 | bytes 10000000 | tf_op jit(solution)/shard_map/pallas_call | solution.py:392
Async XLA Ops:
  0.7 37.3 %copy-start = (bf16[1024,1024]{1,0:T(8,128)(2,1)S(1)}, bf16[1024,1024]{1,0:T(8,128)(2,1)}, u32[]{:S(2)}) copy-start(bf16[1024,1024]{1,0:T(8,128)(2,1)} %constant.5.clone.lag_ref) | copy-start | bytes 6291460

commit v4 on v3

--- a/solution.py
+++ b/solution.py
@@ -18,13 +18,12 @@
 GROUPS = FBINS // GROUP
 PIECES = 4
 CROSS = 1
-TOGETHER = 1
 BATCH = 4
 PIECE_KEY, HOP_KEY, COMPUTE_KEY = 1, 10, 1.5
 
 
-def table(phase):
-    angles = phase.astype(np.float32) * np.float32(2.0 * math.pi / SAMPLES)
+def table(phase, period=SAMPLES):
+    angles = phase.astype(np.float32) * np.float32(2.0 * math.pi / period)
     return np.cos(angles).astype(jnp.bfloat16), (-np.sin(angles)).astype(jnp.bfloat16)
 
 
@@ -39,10 +38,9 @@
     return np.stack(parts)
 
 
-def lag_table_np():
-    bins = bin_order().reshape(GROUPS, GROUP)
-    lags = (np.arange(LAGS) - LAGS // 2)[None, :]
-    return np.concatenate([part for group in bins for part in table(group[:, None] * lags % SAMPLES)], axis=0)
+def lag_tables():
+    bins = bin_order().reshape(-1, 2, BATCH, GROUP).transpose(0, 2, 1, 3).reshape(-1, 1)
+    return table(bins * (2 * np.arange(LAGS // 2) + 1)[None, :] % (2 * SAMPLES), 2 * SAMPLES)
 
 
 def toeplitz(taps):
@@ -264,10 +262,19 @@
             send_own(piece)
 
     for b in range(4):
+        order = 2 * (b % 2 * 128 + iota((segs, 128), 1)) + b // 2
+        angle = (KLO + order).astype(jnp.float32) * (math.pi / SAMPLES)
+        square = angle * angle
+        cosine = 1 - square / 2 * (1 - square / 12 * (1 - square / 30 * (1 - square / 56)))
+        sine = angle * (1 - square / 6 * (1 - square / 20 * (1 - square / 42 * (1 - square / 72))))
         for tile in range(width // 128):
-            own = [
-                [acc[b, part, r * segs : (r + 1) * segs, :] for part in range(2)] for r in range(tile * 4, tile * 4 + 4)
-            ]
+            own = []
+            for r in range(tile * 4, tile * 4 + 4):
+                re, im = (
+                    acc[b, part, r * segs : (r + 1) * segs, :].astype(jnp.bfloat16).astype(jnp.float32)
+                    for part in range(2)
+                )
+                own.append((re * cosine + im * sine, im * cosine - re * sine))
             lanes = slice(tile * 128, (tile + 1) * 128)
             for kind, parts in enumerate(([x for re, im in own for x in (re, im)], [x for re, im in own for x in (im, -re)])):
                 for k, value in enumerate(exchange(parts)):
@@ -293,21 +300,26 @@
         first = piece * per_piece + batch * BATCH
         return [dot(sources[:, k * 256 : (k + 1) * 256], bd[first + k]) for k in range(BATCH)]
 
-    def arrange(values, batch):
+    def arrange(values):
         parts = []
         for tile in range(width // 128):
             lanes = slice(tile * 128, (tile + 1) * 128)
             parts += exchange([(value[:, lanes] * scale[:, lanes]).astype(jnp.bfloat16) for value in values])
-        out_ref[batch] = jnp.transpose(jnp.stack(parts), (1, 0, 2)).reshape(BLOCK * rows, 128)
-        store(batch).start()
-
-    def compute(pieces):
-        for piece in pieces:
-            copy(0, piece, near_sem, core_sem.at[piece], core_peer, 2 * levels).wait_recv()
-        batches = [(piece, batch) for piece in pieces for batch in range(per_piece // BATCH)]
-        values = [crossed(piece, batch) for piece, batch in batches]
-        for (piece, batch), value in zip(batches, values):
-            arrange(value, piece * (per_piece // BATCH) + batch)
+        return parts
+
+    def leave(parts, index):
+        out_ref[index] = jnp.transpose(jnp.stack(parts), (1, 0, 2)).reshape(BLOCK * rows, 128)
+        store(index).start()
+
+    def compute(piece):
+        copy(0, piece, near_sem, core_sem.at[piece], core_peer, 2 * levels).wait_recv()
+        values = [crossed(piece, batch) for batch in range(per_piece // BATCH)]
+        for pair in range(per_piece // BATCH // 2):
+            first, second = (arrange(values[2 * pair + k]) for k in range(2))
+            upper = (iota((BLOCK, 128), 1).astype(jnp.int16) & GROUP) != 0
+            index = (piece * (per_piece // BATCH // 2) + pair) * 2
+            leave([jnp.where(upper, pltpu.roll(b, GROUP, 1), a) for a, b in zip(first, second)], index)
+            leave([jnp.where(upper, b, pltpu.roll(a, 128 - GROUP, 1)) for a, b in zip(first, second)], index + 1)
 
     events = []
     for piece in range(PIECES):
@@ -315,11 +327,10 @@
             if distance:
                 events.append((piece * PIECE_KEY + distance * HOP_KEY, piece, distance, along))
             events.append((piece * PIECE_KEY + (distance + 1) * HOP_KEY, piece, distance, across))
-        if piece % TOGETHER == TOGETHER - 1:
-            events.append((piece * PIECE_KEY + levels * HOP_KEY + COMPUTE_KEY, piece, -1, None))
+        events.append((piece * PIECE_KEY + levels * HOP_KEY + COMPUTE_KEY, piece, -1, None))
     for _, piece, distance, act in sorted(events, key=lambda event: event[:3]):
         if act is None:
-            compute(range(piece + 1 - TOGETHER, piece + 1))
+            compute(piece)
         else:
             each(distance, piece, act)
 
@@ -379,28 +390,39 @@
     )(raw, bandpass[None], whiten_taps, segment_mask, channel_block[None], source_block, jnp.asarray(dft_table()))
 
 
-STEPS = 4
-
-
-def lag_kernel(stacked_ref, lag_ref, out_ref):
-    stacked = jnp.concatenate([stacked_ref[k] for k in range(stacked_ref.shape[0])], axis=1)
-    lagged = dot(stacked, lag_ref[...])
-    out_ref[...] = lagged.astype(jnp.bfloat16).reshape(out_ref.shape)
+STEPS = 2
+
+
+def lag_kernel(stacked_ref, cos_ref, sin_ref, out_ref):
+    sources, rows, lags = out_ref.shape
+    height, half = sources * rows, lags // 2
+    re, im = (
+        jnp.concatenate([stacked_ref[k] for k in range(part, stacked_ref.shape[0], 2)], axis=1) for part in range(2)
+    )
+    even, odd = dot(re, cos_ref[...]), dot(im, sin_ref[...])
+    out_ref[:, :, half:] = (even + odd).astype(jnp.bfloat16).reshape(sources, rows, half)
+    turned = 127 - iota((height, 128), 1)
+    negative = even - odd
+    for first in range(0, half, 128):
+        part = jnp.take_along_axis(negative[:, first : first + 128], turned, axis=1)
+        out_ref[:, :, half - first - 128 : half - first] = part.astype(jnp.bfloat16).reshape(sources, rows, 128)
 
 
 def lag(stacked, rows):
+    vmem = pl.BlockSpec(memory_space=pltpu.VMEM)
     return pl.pallas_call(
         lag_kernel,
         out_shape=jax.ShapeDtypeStruct((BLOCK, rows, LAGS), jnp.bfloat16),
         grid=(STEPS,),
         in_specs=[
             pl.BlockSpec((stacked.shape[0], BLOCK // STEPS * rows, 128), lambda i: (0, i, 0)),
-            pl.BlockSpec(memory_space=pltpu.VMEM),
+            vmem,
+            vmem,
         ],
         out_specs=pl.BlockSpec((BLOCK // STEPS, rows, LAGS), lambda i: (i, 0, 0)),
         compiler_params=pltpu.CompilerParams(vmem_limit_bytes=50 * 2**20),
-        cost_estimate=pl.CostEstimate(flops=4 * 10**9, bytes_accessed=10**7, transcendentals=0),
-    )(stacked, jnp.asarray(lag_table_np()))
+        cost_estimate=pl.CostEstimate(flops=2 * 10**9, bytes_accessed=10**7, transcendentals=0),
+    )(stacked, *(jnp.asarray(part) for part in lag_tables()))
 
 
 def body(count, raw_strain, bandpass, whiten_taps, segment_mask, channel_block, source_block):

time: 45.9 us -> 44.7 us (0.974)
  Pallas kernels: 45 us -> 43.8 us
    pallas_call x1, Pallas kernels: 7.68 us -> 5.72 us  [lag(): pl.pallas_call(lag_kernel, out_shape=jax.ShapeDtypeStruct((BLOCK, rows, L...]
    pallas_call x1, Pallas kernels: 37.3 us -> 38.1 us  [main(): pl.pallas_call(functools.partial(main_kernel, count), out_shape=jax.Shape...]
where the time goes in v4:
time: 44.7 us; the launch traced here: 44.5 us
  Pallas kernels  43.8 us (98%)
  between operations  0.69 us (2%)
    pallas_call x1, Pallas kernels, main(): pl.pallas_call(functools.partial(main_kernel, count), out_shape=jax.Shape...  38.1 us
    pallas_call x1, Pallas kernels, lag(): pl.pallas_call(lag_kernel, out_shape=jax.ShapeDtypeStruct((BLOCK, rows, L...  5.72 us

profile of v4, /device:TPU:1, one launch (start us, length us, event | category | flops | bytes accessed | tf_op | source)
XLA Modules:
  0.0 44.5 jit_solution(4178413339659206480)
XLA Ops:
  0.7 0.0 copy-start
  0.7 0.0 copy-start.1
  0.7 38.1 %shard_map.91.stacked_ref = bf16[8,2048,128]{2,1,0:T(8,128)(2,1)} custom-call(bf16[8,16,4096]{2,1,0:T(8,128)(2,1)} %raw_hbm.1, bf16[1,64]{1,0:T(2,128)(2,1)} %bitcast.3, bf16[16,64]{1,0:T(8,128)(2,1)} %taps_hbm.1, s32[8,256]{1,0:T(8,128)} %mask_hbm.1, s32[1,256]{1,0:T(1,128)} %bitcast.2, s32[1]{0:T(128)S(6)} %copy.10.source_ref, ...), custom_call_target="tpu_custom_call" | custom-call | tf_op jit(solution)/shard_map/pallas_call | solution.py:358
  38.8 0.0 copy-done
  38.8 0.0 copy-done.1
  38.8 5.7 %shard_map.92 = bf16[128,16,1024]{2,1,0:T(8,128)(2,1)} custom-call(bf16[8,2048,128]{2,1,0:T(8,128)(2,1)} %shard_map.91.stacked_ref, bf16[512,512]{1,0:T(8,128)(2,1)S(1)} %copy-done.1, bf16[512,512]{1,0:T(8,128)(2,1)S(1)} %copy-done), custom_call_target="tpu_custom_call" | custom-call | flops 2000000000 | bytes 10000000 | tf_op jit(solution)/shard_map/pallas_call | solution.py:413
Async XLA Ops:
  0.7 38.1 %copy-start = (bf16[512,512]{1,0:T(8,128)(2,1)S(1)}, bf16[512,512]{1,0:T(8,128)(2,1)}, u32[]{:S(2)}) copy-start(bf16[512,512]{1,0:T(8,128)(2,1)} %constant.8.clone.sin_ref) | copy-start | bytes 1572868
  0.7 38.1 %copy-start.1 = (bf16[512,512]{1,0:T(8,128)(2,1)S(1)}, bf16[512,512]{1,0:T(8,128)(2,1)}, u32[]{:S(2)}) copy-start(bf16[512,512]{1,0:T(8,128)(2,1)} %constant.7.clone.cos_ref) | copy-start | bytes 1572868

commit v5 on v4

--- a/solution.py
+++ b/solution.py
@@ -117,8 +117,6 @@
     table_loads = [
         pltpu.make_async_copy(table_hbm.at[b], table_ref.at[b], load_sem.at[1 + b]) for b in range(4)
     ]
-    for load in table_loads:
-        load.start()
 
     def greet(peer):
         pl.semaphore_signal(barrier, inc=1, device_id={"chan": peer}, device_id_type=pl.DeviceIdType.MESH)
@@ -157,6 +155,8 @@
     taps = widen(taps_ref[...])
     blocks = samples // 128
     raw_load.wait()
+    for load in table_loads:
+        load.start()
     power = jnp.zeros((segs * rows, 128), jnp.float32)
     for b in range(blocks):
         if b == 0:
@@ -218,13 +218,13 @@
     def along(far, way, piece):
         arrived(far, 0, piece)
         to_z(far, 0, piece, way < 0)
-        if piece >= CROSS:
+        if piece < PIECES - CROSS:
             to_y(far, piece)
         to_core(far * 4 + side * 2 + core, piece)
 
     def across(far, way, piece):
         arrived(far, 1, piece)
-        if piece < CROSS:
+        if piece >= PIECES - CROSS:
             if way >= 0:
                 to_z(far, 1, piece, False)
             if way <= 0:
@@ -335,7 +335,7 @@
             each(distance, piece, act)
 
     for piece in range(PIECES):
-        crossing = piece < CROSS
+        crossing = piece >= PIECES - CROSS
         copy(0, piece, near_sem, core_sem.at[piece], core_peer, 2 * levels + (1 if crossing else levels)).wait_send()
         each_way = 2 if crossing else 1
 

time: 44.7 us -> 43.9 us (0.982)
  Pallas kernels: 43.8 us -> 43 us
    pallas_call x1, Pallas kernels: 38.1 us -> 37.3 us  [main(): pl.pallas_call(functools.partial(main_kernel, count), out_shape=jax.Shape...]
where the time goes in v5:
time: 43.9 us; the launch traced here: 43.7 us
  Pallas kernels  43 us (98%)
  between operations  0.69 us (2%)
    pallas_call x1, Pallas kernels, main(): pl.pallas_call(functools.partial(main_kernel, count), out_shape=jax.Shape...  37.3 us
    pallas_call x1, Pallas kernels, lag(): pl.pallas_call(lag_kernel, out_shape=jax.ShapeDtypeStruct((BLOCK, rows, L...  5.72 us

profile of v5, /device:TPU:1, one launch (start us, length us, event | category | flops | bytes accessed | tf_op | source)
XLA Modules:
  0.0 43.7 jit_solution(7222854009145551291)
XLA Ops:
  0.7 0.0 copy-start
  0.7 0.0 copy-start.1
  0.7 37.3 %shard_map.91.stacked_ref = bf16[8,2048,128]{2,1,0:T(8,128)(2,1)} custom-call(bf16[8,16,4096]{2,1,0:T(8,128)(2,1)} %raw_hbm.1, bf16[1,64]{1,0:T(2,128)(2,1)} %bitcast.3, bf16[16,64]{1,0:T(8,128)(2,1)} %taps_hbm.1, s32[8,256]{1,0:T(8,128)} %mask_hbm.1, s32[1,256]{1,0:T(1,128)} %bitcast.2, s32[1]{0:T(128)S(6)} %copy.10.source_ref, ...), custom_call_target="tpu_custom_call" | custom-call | tf_op jit(solution)/shard_map/pallas_call | solution.py:358
  38.0 0.0 copy-done
  38.0 0.0 copy-done.1
  38.0 5.7 %shard_map.92 = bf16[128,16,1024]{2,1,0:T(8,128)(2,1)} custom-call(bf16[8,2048,128]{2,1,0:T(8,128)(2,1)} %shard_map.91.stacked_ref, bf16[512,512]{1,0:T(8,128)(2,1)S(1)} %copy-done.1, bf16[512,512]{1,0:T(8,128)(2,1)S(1)} %copy-done), custom_call_target="tpu_custom_call" | custom-call | flops 2000000000 | bytes 10000000 | tf_op jit(solution)/shard_map/pallas_call | solution.py:413
Async XLA Ops:
  0.7 37.3 %copy-start = (bf16[512,512]{1,0:T(8,128)(2,1)S(1)}, bf16[512,512]{1,0:T(8,128)(2,1)}, u32[]{:S(2)}) copy-start(bf16[512,512]{1,0:T(8,128)(2,1)} %constant.8.clone.sin_ref) | copy-start | bytes 1572868
  0.7 37.3 %copy-start.1 = (bf16[512,512]{1,0:T(8,128)(2,1)S(1)}, bf16[512,512]{1,0:T(8,128)(2,1)}, u32[]{:S(2)}) copy-start(bf16[512,512]{1,0:T(8,128)(2,1)} %constant.7.clone.cos_ref) | copy-start | bytes 1572868

commit v6 on v5

--- a/solution.py
+++ b/solution.py
@@ -326,7 +326,8 @@
         for distance in range(levels):
             if distance:
                 events.append((piece * PIECE_KEY + distance * HOP_KEY, piece, distance, along))
-            events.append((piece * PIECE_KEY + (distance + 1) * HOP_KEY, piece, distance, across))
+            hops = distance + 1 if piece >= PIECES - CROSS else max(distance, 2) + 1
+            events.append((piece * PIECE_KEY + hops * HOP_KEY, piece, distance, across))
         events.append((piece * PIECE_KEY + levels * HOP_KEY + COMPUTE_KEY, piece, -1, None))
     for _, piece, distance, act in sorted(events, key=lambda event: event[:3]):
         if act is None:

time: 43.9 us -> 43.4 us (0.989)
    pallas_call x1, Pallas kernels: 37.3 us -> 36.8 us  [main(): pl.pallas_call(functools.partial(main_kernel, count), out_shape=jax.Shape...]
where the time goes in v6:
time: 43.4 us; the launch traced here: 43.3 us
  Pallas kernels  42.6 us (98%)
  between operations  0.69 us (2%)
    pallas_call x1, Pallas kernels, main(): pl.pallas_call(functools.partial(main_kernel, count), out_shape=jax.Shape...  36.8 us
    pallas_call x1, Pallas kernels, lag(): pl.pallas_call(lag_kernel, out_shape=jax.ShapeDtypeStruct((BLOCK, rows, L...  5.72 us

profile of v6, /device:TPU:1, one launch (start us, length us, event | category | flops | bytes accessed | tf_op | source)
XLA Modules:
  0.0 43.3 jit_solution(9547183854452297086)
XLA Ops:
  0.7 0.0 copy-start
  0.7 0.0 copy-start.1
  0.7 36.8 %shard_map.91.stacked_ref = bf16[8,2048,128]{2,1,0:T(8,128)(2,1)} custom-call(bf16[8,16,4096]{2,1,0:T(8,128)(2,1)} %raw_hbm.1, bf16[1,64]{1,0:T(2,128)(2,1)} %bitcast.3, bf16[16,64]{1,0:T(8,128)(2,1)} %taps_hbm.1, s32[8,256]{1,0:T(8,128)} %mask_hbm.1, s32[1,256]{1,0:T(1,128)} %bitcast.2, s32[1]{0:T(128)S(6)} %copy.10.source_ref, ...), custom_call_target="tpu_custom_call" | custom-call | tf_op jit(solution)/shard_map/pallas_call | solution.py:359
  37.5 0.0 copy-done
  37.5 0.0 copy-done.1
  37.5 5.7 %shard_map.92 = bf16[128,16,1024]{2,1,0:T(8,128)(2,1)} custom-call(bf16[8,2048,128]{2,1,0:T(8,128)(2,1)} %shard_map.91.stacked_ref, bf16[512,512]{1,0:T(8,128)(2,1)S(1)} %copy-done.1, bf16[512,512]{1,0:T(8,128)(2,1)S(1)} %copy-done), custom_call_target="tpu_custom_call" | custom-call | flops 2000000000 | bytes 10000000 | tf_op jit(solution)/shard_map/pallas_call | solution.py:414
Async XLA Ops:
  0.7 36.9 %copy-start = (bf16[512,512]{1,0:T(8,128)(2,1)S(1)}, bf16[512,512]{1,0:T(8,128)(2,1)}, u32[]{:S(2)}) copy-start(bf16[512,512]{1,0:T(8,128)(2,1)} %constant.8.clone.sin_ref) | copy-start | bytes 1572868
  0.7 36.9 %copy-start.1 = (bf16[512,512]{1,0:T(8,128)(2,1)S(1)}, bf16[512,512]{1,0:T(8,128)(2,1)}, u32[]{:S(2)}) copy-start(bf16[512,512]{1,0:T(8,128)(2,1)} %constant.7.clone.cos_ref) | copy-start | bytes 1572868

commit v7 on v6

--- a/solution.py
+++ b/solution.py
@@ -210,17 +210,17 @@
         copy(me, piece, near_sem, recv_sem.at[far * 2 + other, piece], y_peer).wait_recv()
 
     def send_own(piece):
+        to_core(me, piece)
         to_z(level, 0, piece, True)
         to_z(level, 0, piece, False)
         to_y(level, piece)
-        to_core(me, piece)
 
     def along(far, way, piece):
         arrived(far, 0, piece)
+        to_core(far * 4 + side * 2 + core, piece)
         to_z(far, 0, piece, way < 0)
         if piece < PIECES - CROSS:
             to_y(far, piece)
-        to_core(far * 4 + side * 2 + core, piece)
 
     def across(far, way, piece):
         arrived(far, 1, piece)

time: 43.4 us -> 43.4 us (level)
  no operation moved by 1% of the time
where the time goes in v7:
time: 43.4 us; the launch traced here: 43.3 us
  Pallas kernels  42.6 us (98%)
  between operations  0.69 us (2%)
    pallas_call x1, Pallas kernels, main(): pl.pallas_call(functools.partial(main_kernel, count), out_shape=jax.Shape...  36.8 us
    pallas_call x1, Pallas kernels, lag(): pl.pallas_call(lag_kernel, out_shape=jax.ShapeDtypeStruct((BLOCK, rows, L...  5.72 us

profile of v7, /device:TPU:1, one launch (start us, length us, event | category | flops | bytes accessed | tf_op | source)
XLA Modules:
  0.0 43.3 jit_solution(12338368957374095173)
XLA Ops:
  0.7 0.0 copy-start
  0.7 0.0 copy-start.1
  0.7 36.8 %shard_map.91.stacked_ref = bf16[8,2048,128]{2,1,0:T(8,128)(2,1)} custom-call(bf16[8,16,4096]{2,1,0:T(8,128)(2,1)} %raw_hbm.1, bf16[1,64]{1,0:T(2,128)(2,1)} %bitcast.3, bf16[16,64]{1,0:T(8,128)(2,1)} %taps_hbm.1, s32[8,256]{1,0:T(8,128)} %mask_hbm.1, s32[1,256]{1,0:T(1,128)} %bitcast.2, s32[1]{0:T(128)S(6)} %copy.10.source_ref, ...), custom_call_target="tpu_custom_call" | custom-call | tf_op jit(solution)/shard_map/pallas_call | solution.py:359
  37.5 0.0 copy-done
  37.5 0.0 copy-done.1
  37.5 5.7 %shard_map.92 = bf16[128,16,1024]{2,1,0:T(8,128)(2,1)} custom-call(bf16[8,2048,128]{2,1,0:T(8,128)(2,1)} %shard_map.91.stacked_ref, bf16[512,512]{1,0:T(8,128)(2,1)S(1)} %copy-done.1, bf16[512,512]{1,0:T(8,128)(2,1)S(1)} %copy-done), custom_call_target="tpu_custom_call" | custom-call | flops 2000000000 | bytes 10000000 | tf_op jit(solution)/shard_map/pallas_call | solution.py:414
Async XLA Ops:
  0.7 36.9 %copy-start = (bf16[512,512]{1,0:T(8,128)(2,1)S(1)}, bf16[512,512]{1,0:T(8,128)(2,1)}, u32[]{:S(2)}) copy-start(bf16[512,512]{1,0:T(8,128)(2,1)} %constant.8.clone.sin_ref) | copy-start | bytes 1572868
  0.7 36.9 %copy-start.1 = (bf16[512,512]{1,0:T(8,128)(2,1)S(1)}, bf16[512,512]{1,0:T(8,128)(2,1)}, u32[]{:S(2)}) copy-start(bf16[512,512]{1,0:T(8,128)(2,1)} %constant.7.clone.cos_ref) | copy-start | bytes 1572868
